TPU v7x, 256 devices: a whole 4x4x8 slice. The times are simulated.
256 devices in a mesh: dp: 64 (over y, z, x_lo), mp: 4 (over x_hi, core).
Axes of the slice: x: 4 (x_hi: 2, x_lo: 2; x = x_hi * 2 + x_lo), y: 4, z: 8, core: 2. Of those that a mesh axis runs over, the one named last changes fastest.
Arguments:
- photo_embedding_matrix: float32 [98304, 1152], P(('dp', 'mp')), may hold values from -1.8 to 1.8
- caption_embedding_matrix: float32 [98304, 1152], P(('dp', 'mp')), may hold values from -1.8 to 1.8
- caption_mate_entry: int32 [98304], P(('dp', 'mp')), may hold values from 0 to 98303, as said below
- sharpness_factor: float32 [1], replicated, may hold values from 0.5 to 2
- affinity_offset: float32 [1], replicated, may hold values from -1 to 1
Outputs:
- grad_images: float32 [98304, 1152], P(('dp', 'mp'))
- text_gradient: float32 [98304, 1152], P(('dp', 'mp'))
Inputs may be any that keep to these rules, and one draw needn't show every extreme that they name: `caption_mate_entry`: partner of row i lies in the same aligned block of 384 rows as i, and within each block the partners are a permutation of that block's rows.
All inputs are finite; a program needn't handle non-finite values.
Results may differ from a plain program's by a relative error of at most 0.0001.
Values sent between devices are 32-bit elements; how exact they have to be, the bound alone decides.
A program may use at most 64 MiB of HBM per device.

v0:
```python
import functools

import jax
import jax.numpy as jnp
from jax import lax
from jax.experimental import pallas as pl
from jax.experimental.pallas import tpu as pltpu
from jax.sharding import PartitionSpec as P

HOPS = 4
PIECES = 12
PARTS = 3
PER = PIECES // PARTS
AHEAD = 3
LAG = 1
TEXT, IMAGE, SIB, A2, A4, B2, B4, A2S, B2S, X4S, PASS_P, PASS_Q = range(12)
SLOTS = 12
NT = (((1,), (1,)), ((), ()))


def split(value):
    high = value.astype(jnp.bfloat16)
    return high, (value - high.astype(jnp.float32)).astype(jnp.bfloat16)


def dot(left, right):
    return jnp.dot(left, right, preferred_element_type=jnp.float32)


def dot_nt(left, right):
    return lax.dot_general(left, right, NT, preferred_element_type=jnp.float32)


def kernel(
    planes, text_ref, image_ref, mate_ref, scale_ref, offset_ref, out_ref,
    buf, high_ref, low_ref, send_sem, recv_sem, load_sem,
):
    rows = text_ref.shape[0]
    piece, part = rows // PIECES, rows // PARTS
    dp, mp = lax.axis_index("dp"), lax.axis_index("mp")
    plane, x_lo = dp // 2, dp % 2
    side, core = mp // 2, mp % 2
    outer = jnp.where(x_lo == side, 1, 0)
    is_outer = x_lo == side
    near, far = side, 1 - side
    type_a2 = jnp.where(is_outer, far, near)
    type_b2 = jnp.where(is_outer, near, far)

    def at(z, lo, hi, c):
        return (z * 2 + lo, hi * 2 + c)

    beside = at(plane, 1 - x_lo, side, core)
    across = at(plane, 1 - x_lo, 1 - side, core)
    sibling = at(plane, x_lo, side, 1 - core)
    up = at((plane + 1) % planes, x_lo, side, core)
    down = at((plane + planes - 1) % planes, x_lo, side, core)

    def pick(flag, yes, no):
        return tuple(jnp.where(flag, a, b) for a, b in zip(yes, no))

    z_near = pick(side == 0, up, down)
    z_far = pick(side == 0, down, up)

    def move(flow, source, target, index, device):
        lines = pl.ds(pl.multiple_of(index * piece, piece), piece)
        return pltpu.make_async_remote_copy(
            src_ref=buf.at[source, lines],
            dst_ref=buf.at[target, lines],
            send_sem=send_sem.at[flow, index],
            recv_sem=recv_sem.at[target, index],
            device_id=device,
            device_id_type=pl.DeviceIdType.MESH,
        )

    def arrived(slot, index):
        move(0, slot, slot, index, sibling).wait_recv()

    first_target = jnp.where(is_outer, A4, PASS_P)
    second_target = jnp.where(is_outer, PASS_Q, A2)
    second_device = pick(is_outer, z_far, across)
    third_source = jnp.where(is_outer, PASS_Q, A4)
    fourth_source = jnp.where(is_outer, PASS_Q, far)

    flows = [
        lambda i: move(0, near, first_target, i, beside),
        lambda i: move(1, far, second_target, i, second_device),
        lambda i: move(2, PASS_P, A2, i, across),
        lambda i: move(3, PASS_P, A4, i, z_near),
        lambda i: move(4, third_source, B2, i, across),
        lambda i: move(5, fourth_source, B4, i, beside),
        lambda i: move(6, core, SIB, i, sibling),
        lambda i: move(7, A2, A2S, i, sibling),
        lambda i: move(8, B2, B2S, i, sibling),
        lambda i: move(9, jnp.where(core == side, B4, A4), X4S, i, sibling),
    ]

    load_text = pltpu.make_async_copy(text_ref, buf.at[TEXT], load_sem.at[0])
    load_image = pltpu.make_async_copy(image_ref, buf.at[IMAGE], load_sem.at[1])
    load_text.start()
    load_image.start()

    barrier = pltpu.get_barrier_semaphore()

    def greet(device):
        pl.semaphore_signal(barrier, inc=1, device_id=device, device_id_type=pl.DeviceIdType.MESH)

    for device in (beside, across, sibling):
        greet(device)

    @pl.when(is_outer)
    def _():
        greet(up)
        greet(down)

    load_text.wait()
    load_image.wait()
    pl.semaphore_wait(barrier, 3 + 2 * outer)

    def issue(step):
        @pl.when(step < PIECES)
        def _():
            flows[0](step).start()
            flows[1](step).start()
            flows[6](step).start()

        @pl.when((step >= PIECES) & (step < 2 * PIECES))
        def _():
            index = step - PIECES

            @pl.when(is_outer)
            def _():
                arrived(PASS_Q, index)

            flows[4](index).start()
            flows[5](index).start()

    lax.fori_loop(0, AHEAD, lambda i, c: (issue(i), c)[1], 0)

    scale = scale_ref[0]
    offset = offset_ref[0]
    share = scale * jnp.float32(1.0 / (HOPS + 1))

    for kind, slot in ((0, IMAGE), (1, TEXT)):
        high, low = split(buf[slot])
        high_ref[kind] = high
        low_ref[kind] = low
    logits = dot_nt(high_ref[1], high_ref[0])
    logits += dot_nt(high_ref[1], low_ref[0])
    logits += dot_nt(low_ref[1], high_ref[0])
    mine = (dp * 4 + mp) * rows
    line = lax.broadcasted_iota(jnp.int32, (rows, rows), 0) + mine
    sign = jnp.where(line == mate_ref[...], jnp.float32(1.0), jnp.float32(-1.0))
    coef = -sign * jax.nn.sigmoid(-sign * (scale * logits + offset)) * share
    for kind, tile in ((1, coef), (0, coef.T)):
        high, low = split(tile)
        total = dot(high, high_ref[1 - kind])
        total += dot(high, low_ref[1 - kind])
        total += dot(low, high_ref[1 - kind])
        out_ref[kind] = total

    def multiply(slot, kind, index):
        block = buf[slot, pl.ds(pl.multiple_of(index * part, part), part), :]
        high, low = split(block)
        both = jnp.concatenate([high, low], axis=0)
        twice = dot_nt(high_ref[kind], both)
        logits = twice[:, :part] + twice[:, part:] + dot_nt(low_ref[kind], high)
        coef = jax.nn.sigmoid(scale * logits + offset) * share
        coef_high, coef_low = split(coef)
        out_ref[kind] += dot(
            jnp.concatenate([coef_high, coef_low, coef_high], axis=1),
            jnp.concatenate([high, high, low], axis=0),
        )

    def step(i, carry):
        issue(i + AHEAD)

        @pl.when(is_outer & (i < PIECES))
        def _():
            arrived(PASS_P, i)
            flows[2](i).start()
            flows[3](i).start()

        late = i - LAG

        @pl.when((late >= 0) & (late < PIECES))
        def _():
            arrived(A2, late)
            flows[7](late).start()
            arrived(A4, late)

            @pl.when(core != side)
            def _():
                flows[9](late).start()

        @pl.when((late >= PIECES) & (late < 2 * PIECES))
        def _():
            index = late - PIECES
            arrived(B2, index)
            flows[8](index).start()
            arrived(B4, index)

            @pl.when(core == side)
            def _():
                flows[9](index).start()

        item = late - PER

        @pl.when(item >= 0)
        def _():
            half = item // PIECES
            index = item // PER - half * PARTS
            turn = item % PER
            spare = jnp.where((core == side) == (half == 0), X4S, SIB)
            slot = jnp.where(
                half == 0,
                jnp.where(turn == 0, A2, jnp.where(turn == 1, A4, jnp.where(turn == 2, A2S, spare))),
                jnp.where(turn == 0, B2, jnp.where(turn == 1, B4, jnp.where(turn == 2, B2S, spare))),
            )
            type_2 = jnp.where(half == 0, type_a2, type_b2)
            type_4 = jnp.where(half == 0, near, far)
            kind = jnp.where(
                turn % 2 == 0, type_2, jnp.where((turn == 3) & (spare == SIB), 1 - core, type_4)
            )

            @pl.when(turn >= 2)
            def _():
                for k in range(PER):
                    arrived(slot, index * PER + k)

            multiply(slot, kind, index)

        return carry

    lax.fori_loop(0, 2 * PIECES + LAG + PER, step, 0)

    def finish(i, carry):
        for flow in (0, 1, 4, 5, 6, 7, 8, 9):
            flows[flow](i).wait_send()

        @pl.when(is_outer)
        def _():
            flows[2](i).wait_send()
            flows[3](i).wait_send()

        return carry

    lax.fori_loop(0, PIECES, finish, 0)


def body(photo_embedding_matrix, caption_embedding_matrix, caption_mate_entry, sharpness_factor, affinity_offset):
    rows, width = photo_embedding_matrix.shape
    planes = lax.axis_size("dp") // 2
    both = pl.pallas_call(
        functools.partial(kernel, planes),
        out_shape=jax.ShapeDtypeStruct((2, rows, width), jnp.float32),
        in_specs=[
            pl.BlockSpec(memory_space=pl.ANY),
            pl.BlockSpec(memory_space=pl.ANY),
            pl.BlockSpec(memory_space=pltpu.VMEM),
            pl.BlockSpec(memory_space=pltpu.SMEM),
            pl.BlockSpec(memory_space=pltpu.SMEM),
        ],
        out_specs=pl.BlockSpec(memory_space=pltpu.VMEM),
        scratch_shapes=[
            pltpu.VMEM((SLOTS, rows, width), jnp.float32),
            pltpu.VMEM((2, rows, width), jnp.bfloat16),
            pltpu.VMEM((2, rows, width), jnp.bfloat16),
            pltpu.SemaphoreType.DMA((10, PIECES)),
            pltpu.SemaphoreType.DMA((SLOTS, PIECES)),
            pltpu.SemaphoreType.DMA((2,)),
        ],
        compiler_params=pltpu.CompilerParams(
            collective_id=0, has_side_effects=True, vmem_limit_bytes=56 * 1024 * 1024
        ),
        cost_estimate=pl.CostEstimate(
            flops=57 * 2 * rows * rows * width,
            bytes_accessed=16 * rows * width,
            transcendentals=9 * rows * rows,
        ),
    )(
        caption_embedding_matrix,
        photo_embedding_matrix,
        caption_mate_entry.reshape(1, rows),
        sharpness_factor,
        affinity_offset,
    )
    return both[0], both[1]


def solution(mesh):
    in_specs = (P(("dp", "mp"), None), P(("dp", "mp"), None), P(("dp", "mp")), P(), P())
    out_specs = (P(("dp", "mp"), None), P(("dp", "mp"), None))
    return jax.shard_map(body, mesh=mesh, in_specs=in_specs, out_specs=out_specs, check_vma=False)
```

profile of v0, /device:TPU:1, one launch (start us, length us, event | category | flops | bytes accessed | tf_op | source)
XLA Modules:
  0.0 111.5 jit_solution(8230261616862154943)
XLA Ops:
  1.9 1.2 %reshape.7.mate_ref = s32[1,384]{1,0:T(1,128)} reshape(s32[384]{0:T(512)} %param.7) | data formatting | bytes 3072 | tf_op jit(solution)/shard_map/reshape | solution.py:283
  3.2 104.3 %shard_map.68 = f32[2,384,1152]{2,1,0:T(8,128)} custom-call(f32[384,1152]{1,0:T(8,128)} %text_ref.1, f32[384,1152]{1,0:T(8,128)} %image_ref.1, s32[1,384]{1,0:T(1,128)} %reshape.7.mate_ref, f32[1]{0:T(128)S(6)} %copy.7.scale_ref, f32[1]{0:T(128)S(6)} %copy.8.offset_ref), custom_call_target="tpu_custom_call" | custom-call | flops 19365101568 | bytes 7077888 | tf_op jit(solution)/shard_map/pallas_call | solution.py:253
  107.5 4.0 %slice_bitcast_fusion = (f32[384,1152]{1,0:T(8,128)}, f32[384,1152]{1,0:T(8,128)}) fusion(f32[2,384,1152]{2,1,0:T(8,128)} %shard_map.68), kind=kLoop, calls=%fused_computation | loop fusion | bytes 7077888 | tf_op jit(solution)/shard_map/squeeze | solution.py:287
where the time goes:
time: 113 us; the launch traced here: 112 us
  Pallas kernels  104 us (92%)
  local copies, waits for them, and re-layouts  5.27 us (5%)
  between operations  1.93 us (2%)
    pallas_call x1, Pallas kernels, body(): pl.pallas_call(functools.partial(kernel, planes), out_shape=jax.ShapeDtyp...  104 us
    squeeze x1, local copies, waits for them, and re-layouts, body(): return (both[0], both[1])  4.03 us

commit v1 on v0

--- a/solution.py
+++ b/solution.py
@@ -9,10 +9,8 @@
 
 HOPS = 4
 PIECES = 12
-PARTS = 3
-PER = PIECES // PARTS
-AHEAD = 3
-LAG = 1
+AHEAD = 2
+LAG = 2
 TEXT, IMAGE, SIB, A2, A4, B2, B4, A2S, B2S, X4S, PASS_P, PASS_Q = range(12)
 SLOTS = 12
 NT = (((1,), (1,)), ((), ()))
@@ -33,10 +31,10 @@
 
 def kernel(
     planes, text_ref, image_ref, mate_ref, scale_ref, offset_ref, out_ref,
-    buf, high_ref, low_ref, send_sem, recv_sem, load_sem,
+    buf, high_ref, low_ref, mate_buf, send_sem, recv_sem, load_sem,
 ):
     rows = text_ref.shape[0]
-    piece, part = rows // PIECES, rows // PARTS
+    piece = rows // PIECES
     dp, mp = lax.axis_index("dp"), lax.axis_index("mp")
     plane, x_lo = dp // 2, dp % 2
     side, core = mp // 2, mp % 2
@@ -96,8 +94,10 @@
 
     load_text = pltpu.make_async_copy(text_ref, buf.at[TEXT], load_sem.at[0])
     load_image = pltpu.make_async_copy(image_ref, buf.at[IMAGE], load_sem.at[1])
+    load_mate = pltpu.make_async_copy(mate_ref, mate_buf, load_sem.at[2])
     load_text.start()
     load_image.start()
+    load_mate.start()
 
     barrier = pltpu.get_barrier_semaphore()
 
@@ -112,8 +112,10 @@
         greet(up)
         greet(down)
 
+    out_ref[...] = jnp.zeros_like(out_ref)
     load_text.wait()
     load_image.wait()
+    load_mate.wait()
     pl.semaphore_wait(barrier, 3 + 2 * outer)
 
     def issue(step):
@@ -144,26 +146,29 @@
         high, low = split(buf[slot])
         high_ref[kind] = high
         low_ref[kind] = low
-    logits = dot_nt(high_ref[1], high_ref[0])
-    logits += dot_nt(high_ref[1], low_ref[0])
-    logits += dot_nt(low_ref[1], high_ref[0])
-    mine = (dp * 4 + mp) * rows
-    line = lax.broadcasted_iota(jnp.int32, (rows, rows), 0) + mine
-    sign = jnp.where(line == mate_ref[...], jnp.float32(1.0), jnp.float32(-1.0))
-    coef = -sign * jax.nn.sigmoid(-sign * (scale * logits + offset)) * share
-    for kind, tile in ((1, coef), (0, coef.T)):
-        high, low = split(tile)
-        total = dot(high, high_ref[1 - kind])
-        total += dot(high, low_ref[1 - kind])
-        total += dot(low, high_ref[1 - kind])
-        out_ref[kind] = total
-
-    def multiply(slot, kind, index):
-        block = buf[slot, pl.ds(pl.multiple_of(index * part, part), part), :]
+
+    def diagonal():
+        logits = dot_nt(high_ref[1], high_ref[0])
+        logits += dot_nt(high_ref[1], low_ref[0])
+        logits += dot_nt(low_ref[1], high_ref[0])
+        mine = (dp * 4 + mp) * rows
+        line = lax.broadcasted_iota(jnp.int32, (rows, rows), 0) + mine
+        sign = jnp.where(line == mate_buf[...].reshape(1, rows), jnp.float32(1.0), jnp.float32(-1.0))
+        coef = -sign * jax.nn.sigmoid(-sign * (scale * logits + offset)) * share
+        for kind, tile in ((1, coef), (0, coef.T)):
+            high, low = split(tile)
+            total = dot(high, high_ref[1 - kind])
+            total += dot(high, low_ref[1 - kind])
+            total += dot(low, high_ref[1 - kind])
+            out_ref[kind] += total
+
+    def multiply(one, other, kind, index):
+        lines = pl.ds(pl.multiple_of(index * 2 * piece, 2 * piece), 2 * piece)
+        block = jnp.concatenate([buf[one, lines], buf[other, lines]], axis=0)
         high, low = split(block)
         both = jnp.concatenate([high, low], axis=0)
         twice = dot_nt(high_ref[kind], both)
-        logits = twice[:, :part] + twice[:, part:] + dot_nt(low_ref[kind], high)
+        logits = twice[:, : 4 * piece] + twice[:, 4 * piece :] + dot_nt(low_ref[kind], high)
         coef = jax.nn.sigmoid(scale * logits + offset) * share
         coef_high, coef_low = split(coef)
         out_ref[kind] += dot(
@@ -180,6 +185,23 @@
             flows[2](i).start()
             flows[3](i).start()
 
+        item = i - 2 - LAG
+
+        @pl.when(item >= 0)
+        def _():
+            half = item // PIECES
+            index = (item - half * PIECES) // 2
+            spare = jnp.where((core == side) == (half == 0), X4S, SIB)
+            first = item % 2 == 0
+            one = jnp.where(half == 0, jnp.where(first, A2, A4), jnp.where(first, B2, B4))
+            other = jnp.where(first, jnp.where(half == 0, A2S, B2S), spare)
+            kind = jnp.where(
+                first, jnp.where(half == 0, type_a2, type_b2), jnp.where(half == 0, near, far)
+            )
+            arrived(other, 2 * index)
+            arrived(other, 2 * index + 1)
+            multiply(one, other, kind, index)
+
         late = i - LAG
 
         @pl.when((late >= 0) & (late < PIECES))
@@ -203,35 +225,13 @@
             def _():
                 flows[9](index).start()
 
-        item = late - PER
-
-        @pl.when(item >= 0)
-        def _():
-            half = item // PIECES
-            index = item // PER - half * PARTS
-            turn = item % PER
-            spare = jnp.where((core == side) == (half == 0), X4S, SIB)
-            slot = jnp.where(
-                half == 0,
-                jnp.where(turn == 0, A2, jnp.where(turn == 1, A4, jnp.where(turn == 2, A2S, spare))),
-                jnp.where(turn == 0, B2, jnp.where(turn == 1, B4, jnp.where(turn == 2, B2S, spare))),
-            )
-            type_2 = jnp.where(half == 0, type_a2, type_b2)
-            type_4 = jnp.where(half == 0, near, far)
-            kind = jnp.where(
-                turn % 2 == 0, type_2, jnp.where((turn == 3) & (spare == SIB), 1 - core, type_4)
-            )
-
-            @pl.when(turn >= 2)
-            def _():
-                for k in range(PER):
-                    arrived(slot, index * PER + k)
-
-            multiply(slot, kind, index)
+        @pl.when(i == PIECES + 1)
+        def _():
+            diagonal()
 
         return carry
 
-    lax.fori_loop(0, 2 * PIECES + LAG + PER, step, 0)
+    lax.fori_loop(0, 2 * PIECES + LAG + 2, step, 0)
 
     def finish(i, carry):
         for flow in (0, 1, 4, 5, 6, 7, 8, 9):
@@ -252,11 +252,11 @@
     planes = lax.axis_size("dp") // 2
     both = pl.pallas_call(
         functools.partial(kernel, planes),
-        out_shape=jax.ShapeDtypeStruct((2, rows, width), jnp.float32),
+        out_shape=pltpu.VMEM((2, rows, width), jnp.float32),
         in_specs=[
-            pl.BlockSpec(memory_space=pl.ANY),
-            pl.BlockSpec(memory_space=pl.ANY),
-            pl.BlockSpec(memory_space=pltpu.VMEM),
+            pl.BlockSpec(memory_space=pltpu.HBM),
+            pl.BlockSpec(memory_space=pltpu.HBM),
+            pl.BlockSpec(memory_space=pltpu.HBM),
             pl.BlockSpec(memory_space=pltpu.SMEM),
             pl.BlockSpec(memory_space=pltpu.SMEM),
         ],
@@ -265,12 +265,13 @@
             pltpu.VMEM((SLOTS, rows, width), jnp.float32),
             pltpu.VMEM((2, rows, width), jnp.bfloat16),
             pltpu.VMEM((2, rows, width), jnp.bfloat16),
+            pltpu.VMEM((rows,), jnp.int32),
             pltpu.SemaphoreType.DMA((10, PIECES)),
             pltpu.SemaphoreType.DMA((SLOTS, PIECES)),
-            pltpu.SemaphoreType.DMA((2,)),
+            pltpu.SemaphoreType.DMA((3,)),
         ],
         compiler_params=pltpu.CompilerParams(
-            collective_id=0, has_side_effects=True, vmem_limit_bytes=56 * 1024 * 1024
+            collective_id=0, has_side_effects=True, vmem_limit_bytes=48 * 1024 * 1024
         ),
         cost_estimate=pl.CostEstimate(
             flops=57 * 2 * rows * rows * width,
@@ -278,9 +279,9 @@
             transcendentals=9 * rows * rows,
         ),
     )(
-        caption_embedding_matrix,
-        photo_embedding_matrix,
-        caption_mate_entry.reshape(1, rows),
+        pltpu.with_memory_space_constraint(caption_embedding_matrix, pltpu.HBM),
+        pltpu.with_memory_space_constraint(photo_embedding_matrix, pltpu.HBM),
+        pltpu.with_memory_space_constraint(caption_mate_entry, pltpu.HBM),
         sharpness_factor,
         affinity_offset,
     )

time: 113 us -> 99.8 us (0.88); the launches traced: 112 us -> 99.7 us
  Pallas kernels: 104 us -> 95.8 us
  local copies, waits for them, and re-layouts: 5.27 us -> 2.02 us
    pallas_call x1, Pallas kernels: 104 us -> 95.8 us  [body(): pl.pallas_call(functools.partial(kernel, planes), out_shape=pltpu.VMEM((2...]
    squeeze x1, local copies, waits for them, and re-layouts: 4.03 us -> 2.02 us  [body(): return (both[0], both[1])]
    reshape x1 -> x0, local copies, waits for them, and re-layouts: 1.25 us -> none  [body(): caption_mate_entry.reshape(1, rows)]
where the time goes in v1:
time: 99.8 us; the launch traced here: 99.7 us
  Pallas kernels  95.8 us (96%)
  local copies, waits for them, and re-layouts  2.02 us (2%)
  between operations  1.93 us (2%)
    pallas_call x1, Pallas kernels, body(): pl.pallas_call(functools.partial(kernel, planes), out_shape=pltpu.VMEM((2...  95.8 us
    squeeze x1, local copies, waits for them, and re-layouts, body(): return (both[0], both[1])  2.02 us

profile of v1, /device:TPU:1, one launch (start us, length us, event | category | flops | bytes accessed | tf_op | source)
XLA Modules:
  0.0 99.7 jit_solution(9772523744898924508)
XLA Ops:
  1.9 95.8 %shard_map.68 = f32[2,384,1152]{2,1,0:T(8,128)S(1)} custom-call(f32[384,1152]{1,0:T(8,128)} %text_ref.1, f32[384,1152]{1,0:T(8,128)} %image_ref.1, s32[384]{0:T(512)} %mate_ref.1, f32[1]{0:T(128)S(6)} %copy.7.scale_ref, f32[1]{0:T(128)S(6)} %copy.8.offset_ref), custom_call_target="tpu_custom_call" | custom-call | flops 19365101568 | bytes 7077888 | tf_op jit(solution)/shard_map/pallas_call | solution.py:253
  97.7 2.0 %slice_bitcast_fusion = (f32[384,1152]{1,0:T(8,128)}, f32[384,1152]{1,0:T(8,128)}) fusion(f32[2,384,1152]{2,1,0:T(8,128)S(1)} %shard_map.68), kind=kLoop, calls=%fused_computation | loop fusion | bytes 7077888 | tf_op jit(solution)/shard_map/squeeze | solution.py:288

commit v2 on v1

--- a/solution.py
+++ b/solution.py
@@ -10,7 +10,12 @@
 HOPS = 4
 PIECES = 12
 AHEAD = 2
-LAG = 2
+LAG_INNER = 2
+LAG_OUTER = 4
+TRAIL = 1
+SLIVERS = 2
+EARLY = 1
+EARLY_AT = 6
 TEXT, IMAGE, SIB, A2, A4, B2, B4, A2S, B2S, X4S, PASS_P, PASS_Q = range(12)
 SLOTS = 12
 NT = (((1,), (1,)), ((), ()))
@@ -31,15 +36,15 @@
 
 def kernel(
     planes, text_ref, image_ref, mate_ref, scale_ref, offset_ref, out_ref,
-    buf, high_ref, low_ref, mate_buf, send_sem, recv_sem, load_sem,
+    buf, high_ref, low_ref, mate_buf, send_sem, recv_sem, load_sem, sliver_sem, go_sem,
 ):
     rows = text_ref.shape[0]
     piece = rows // PIECES
     dp, mp = lax.axis_index("dp"), lax.axis_index("mp")
     plane, x_lo = dp // 2, dp % 2
     side, core = mp // 2, mp % 2
-    outer = jnp.where(x_lo == side, 1, 0)
     is_outer = x_lo == side
+    lag = jnp.where(is_outer, LAG_OUTER, LAG_INNER)
     near, far = side, 1 - side
     type_a2 = jnp.where(is_outer, far, near)
     type_b2 = jnp.where(is_outer, near, far)
@@ -101,42 +106,108 @@
 
     barrier = pltpu.get_barrier_semaphore()
 
-    def greet(device):
-        pl.semaphore_signal(barrier, inc=1, device_id=device, device_id_type=pl.DeviceIdType.MESH)
-
-    for device in (beside, across, sibling):
-        greet(device)
+    def signal(semaphore, device):
+        pl.semaphore_signal(semaphore, inc=1, device_id=device, device_id_type=pl.DeviceIdType.MESH)
 
     @pl.when(is_outer)
     def _():
-        greet(up)
-        greet(down)
+        signal(barrier, beside)
+        signal(barrier, at(plane, 1 - x_lo, side, 1 - core))
+        signal(barrier, at(plane, x_lo, 1 - side, core))
+        signal(barrier, up)
+        signal(barrier, down)
+
+    @pl.when(x_lo != side)
+    def _():
+        signal(barrier, across)
+        signal(barrier, sibling)
+        pl.semaphore_wait(barrier, 5)
+        signal(go_sem, beside)
+
+    @pl.when(is_outer)
+    def _():
+        pl.semaphore_wait(go_sem, 1)
+
+    def begin(ref, flow, target, index, device):
+        lines = pl.ds(index * piece, piece)
+        pltpu.make_async_remote_copy(
+            src_ref=ref.at[lines],
+            dst_ref=buf.at[target, lines],
+            send_sem=send_sem.at[flow, index],
+            recv_sem=recv_sem.at[target, index],
+            device_id=device,
+            device_id_type=pl.DeviceIdType.MESH,
+        ).start()
+
+    thin = piece // SLIVERS
+
+    def sliver(ref, flow, target, index, part, recv, device):
+        lines = pl.ds(pl.multiple_of(index * piece + part * thin, thin), thin)
+        return pltpu.make_async_remote_copy(
+            src_ref=ref.at[lines],
+            dst_ref=buf.at[target, lines],
+            send_sem=send_sem.at[flow, index],
+            recv_sem=recv,
+            device_id=device,
+            device_id_type=pl.DeviceIdType.MESH,
+        )
+
+    def begin_slivers(ref, index):
+        for part in range(SLIVERS):
+            sliver(ref, 0, PASS_P, index, part, sliver_sem.at[index * SLIVERS + part], beside).start()
+
+    def relay(index):
+        for part in range(SLIVERS):
+            source = buf.at[PASS_P]
+            sliver(source, 2, PASS_P, index, part, sliver_sem.at[index * SLIVERS + part], across).wait_recv()
+            sliver(source, 2, A2, index, part, recv_sem.at[A2, index], across).start()
+
+    for which, near_ref, far_ref in ((0, text_ref, image_ref), (1, image_ref, text_ref)):
+
+        @pl.when((side == which) & is_outer)
+        def _(near_ref=near_ref):
+            for index in range(AHEAD):
+                begin(near_ref, 0, A4, index, beside)
+
+        @pl.when((side == which) & (x_lo != side))
+        def _(near_ref=near_ref, far_ref=far_ref):
+            for index in range(AHEAD):
+                begin_slivers(near_ref, index)
+                begin(far_ref, 1, A2, index, across)
 
     out_ref[...] = jnp.zeros_like(out_ref)
+
+    @pl.when(is_outer)
+    def _():
+        relay(0)
+
     load_text.wait()
     load_image.wait()
     load_mate.wait()
-    pl.semaphore_wait(barrier, 3 + 2 * outer)
 
     def issue(step):
-        @pl.when(step < PIECES)
+        @pl.when((step < PIECES) & is_outer)
         def _():
             flows[0](step).start()
+
+        @pl.when((step < PIECES) & (x_lo != side))
+        def _():
+            begin_slivers(buf.at[near], step)
             flows[1](step).start()
-            flows[6](step).start()
 
         @pl.when((step >= PIECES) & (step < 2 * PIECES))
         def _():
             index = step - PIECES
 
-            @pl.when(is_outer)
+            @pl.when(is_outer & (index >= EARLY))
             def _():
                 arrived(PASS_Q, index)
 
-            flows[4](index).start()
+            @pl.when((x_lo != side) | (index >= EARLY))
+            def _():
+                flows[4](index).start()
+
             flows[5](index).start()
-
-    lax.fori_loop(0, AHEAD, lambda i, c: (issue(i), c)[1], 0)
 
     scale = scale_ref[0]
     offset = offset_ref[0]
@@ -179,15 +250,31 @@
     def step(i, carry):
         issue(i + AHEAD)
 
-        @pl.when(is_outer & (i < PIECES))
-        def _():
-            arrived(PASS_P, i)
-            flows[2](i).start()
-            flows[3](i).start()
-
-        item = i - 2 - LAG
-
-        @pl.when(item >= 0)
+        @pl.when(i < PIECES)
+        def _():
+            flows[6](i).start()
+
+        @pl.when(is_outer & (i >= 1) & (i < PIECES))
+        def _():
+            relay(i)
+
+        @pl.when(is_outer & (i == TRAIL))
+        def _():
+            pl.semaphore_wait(barrier, 2)
+
+        @pl.when(is_outer & (i >= TRAIL) & (i < PIECES + TRAIL))
+        def _():
+            flows[1](i - TRAIL).start()
+            flows[3](i - TRAIL).start()
+
+        @pl.when(is_outer & (i >= EARLY_AT) & (i < EARLY_AT + EARLY))
+        def _():
+            arrived(PASS_Q, i - EARLY_AT)
+            flows[4](i - EARLY_AT).start()
+
+        item = i - 2 - lag
+
+        @pl.when((item >= 0) & (item < 2 * PIECES))
         def _():
             half = item // PIECES
             index = (item - half * PIECES) // 2
@@ -202,7 +289,7 @@
             arrived(other, 2 * index + 1)
             multiply(one, other, kind, index)
 
-        late = i - LAG
+        late = i - lag
 
         @pl.when((late >= 0) & (late < PIECES))
         def _():
@@ -231,7 +318,7 @@
 
         return carry
 
-    lax.fori_loop(0, 2 * PIECES + LAG + 2, step, 0)
+    lax.fori_loop(0, 2 * PIECES + LAG_OUTER + 2, step, 0)
 
     def finish(i, carry):
         for flow in (0, 1, 4, 5, 6, 7, 8, 9):
@@ -269,6 +356,8 @@
             pltpu.SemaphoreType.DMA((10, PIECES)),
             pltpu.SemaphoreType.DMA((SLOTS, PIECES)),
             pltpu.SemaphoreType.DMA((3,)),
+            pltpu.SemaphoreType.DMA((PIECES * SLIVERS,)),
+            pltpu.SemaphoreType.REGULAR,
         ],
         compiler_params=pltpu.CompilerParams(
             collective_id=0, has_side_effects=True, vmem_limit_bytes=48 * 1024 * 1024

time: 99.8 us -> 96.7 us (0.969)
  Pallas kernels: 95.8 us -> 92.6 us
    pallas_call x1, Pallas kernels: 95.8 us -> 92.6 us  [body(): pl.pallas_call(functools.partial(kernel, planes), out_shape=pltpu.VMEM((2...]
where the time goes in v2:
time: 96.7 us; the launch traced here: 96.6 us
  Pallas kernels  92.6 us (96%)
  local copies, waits for them, and re-layouts  2.02 us (2%)
  between operations  1.93 us (2%)
    pallas_call x1, Pallas kernels, body(): pl.pallas_call(functools.partial(kernel, planes), out_shape=pltpu.VMEM((2...  92.6 us
    squeeze x1, local copies, waits for them, and re-layouts, body(): return (both[0], both[1])  2.02 us

profile of v2, /device:TPU:1, one launch (start us, length us, event | category | flops | bytes accessed | tf_op | source)
XLA Modules:
  0.0 96.6 jit_solution(4564103218291743004)
XLA Ops:
  1.9 92.6 %shard_map.68 = f32[2,384,1152]{2,1,0:T(8,128)S(1)} custom-call(f32[384,1152]{1,0:T(8,128)} %text_ref.1, f32[384,1152]{1,0:T(8,128)} %image_ref.1, s32[384]{0:T(512)} %mate_ref.1, f32[1]{0:T(128)S(6)} %copy.7.scale_ref, f32[1]{0:T(128)S(6)} %copy.8.offset_ref), custom_call_target="tpu_custom_call" | custom-call | flops 19365101568 | bytes 7077888 | tf_op jit(solution)/shard_map/pallas_call | solution.py:340
  94.6 2.0 %slice_bitcast_fusion = (f32[384,1152]{1,0:T(8,128)}, f32[384,1152]{1,0:T(8,128)}) fusion(f32[2,384,1152]{2,1,0:T(8,128)S(1)} %shard_map.68), kind=kLoop, calls=%fused_computation | loop fusion | bytes 7077888 | tf_op jit(solution)/shard_map/squeeze | solution.py:377

commit v3 on v2

--- a/solution.py
+++ b/solution.py
@@ -12,10 +12,12 @@
 AHEAD = 2
 LAG_INNER = 2
 LAG_OUTER = 4
-TRAIL = 1
+TRAIL = 0
 SLIVERS = 2
 EARLY = 1
 EARLY_AT = 6
+DETOUR = 3
+DETOUR_AT = 7
 TEXT, IMAGE, SIB, A2, A4, B2, B4, A2S, B2S, X4S, PASS_P, PASS_Q = range(12)
 SLOTS = 12
 NT = (((1,), (1,)), ((), ()))
@@ -156,6 +158,38 @@
         for part in range(SLIVERS):
             sliver(ref, 0, PASS_P, index, part, sliver_sem.at[index * SLIVERS + part], beside).start()
 
+    last = PIECES - 1
+    kept = piece - piece * DETOUR // 4
+
+    def detour(source, flow, target, recv, device):
+        lines = pl.ds(last * piece + kept, piece - kept)
+        return pltpu.make_async_remote_copy(
+            src_ref=buf.at[source, lines],
+            dst_ref=buf.at[target, lines],
+            send_sem=send_sem.at[flow, last],
+            recv_sem=recv,
+            device_id=device,
+            device_id_type=pl.DeviceIdType.MESH,
+        )
+
+    out_way = detour(near, 2, PASS_P, recv_sem.at[PASS_P, last], across)
+    in_way = detour(PASS_P, 3, A2, recv_sem.at[A2, last], beside)
+    lines_kept = pl.ds(last * piece, kept)
+    straight = pltpu.make_async_remote_copy(
+        src_ref=buf.at[PASS_P, lines_kept],
+        dst_ref=buf.at[A2, lines_kept],
+        send_sem=send_sem.at[2, last],
+        recv_sem=recv_sem.at[A2, last],
+        device_id=across,
+        device_id_type=pl.DeviceIdType.MESH,
+    )
+
+    def relay_last():
+        for part in range(SLIVERS):
+            recv = sliver_sem.at[last * SLIVERS + part]
+            sliver(buf.at[PASS_P], 2, PASS_P, last, part, recv, across).wait_recv()
+        straight.start()
+
     def relay(index):
         for part in range(SLIVERS):
             source = buf.at[PASS_P]
@@ -254,9 +288,22 @@
         def _():
             flows[6](i).start()
 
-        @pl.when(is_outer & (i >= 1) & (i < PIECES))
+        @pl.when(is_outer & (i >= 1) & (i < last))
         def _():
             relay(i)
+
+        @pl.when(is_outer & (i == last))
+        def _():
+            relay_last()
+
+        @pl.when((x_lo != side) & (i == DETOUR_AT))
+        def _():
+            out_way.start()
+
+        @pl.when((x_lo != side) & (i == DETOUR_AT + 3))
+        def _():
+            out_way.wait_recv()
+            in_way.start()
 
         @pl.when(is_outer & (i == TRAIL))
         def _():
@@ -326,12 +373,24 @@
 
         @pl.when(is_outer)
         def _():
+            flows[3](i).wait_send()
+
+        @pl.when(is_outer & (i < last))
+        def _():
             flows[2](i).wait_send()
-            flows[3](i).wait_send()
 
         return carry
 
     lax.fori_loop(0, PIECES, finish, 0)
+
+    @pl.when(is_outer)
+    def _():
+        straight.wait_send()
+
+    @pl.when(x_lo != side)
+    def _():
+        out_way.wait_send()
+        in_way.wait_send()
 
 
 def body(photo_embedding_matrix, caption_embedding_matrix, caption_mate_entry, sharpness_factor, affinity_offset):

time: 96.7 us -> 95 us (0.982)
  Pallas kernels: 92.6 us -> 90.9 us
    pallas_call x1, Pallas kernels: 92.6 us -> 90.9 us  [body(): pl.pallas_call(functools.partial(kernel, planes), out_shape=pltpu.VMEM((2...]
where the time goes in v3:
time: 95 us; the launch traced here: 94.9 us
  Pallas kernels  90.9 us (96%)
  local copies, waits for them, and re-layouts  2.02 us (2%)
  between operations  1.93 us (2%)
    pallas_call x1, Pallas kernels, body(): pl.pallas_call(functools.partial(kernel, planes), out_shape=pltpu.VMEM((2...  90.9 us
    squeeze x1, local copies, waits for them, and re-layouts, body(): return (both[0], both[1])  2.02 us

profile of v3, /device:TPU:1, one launch (start us, length us, event | category | flops | bytes accessed | tf_op | source)
XLA Modules:
  0.0 94.9 jit_solution(12551083793931033130)
XLA Ops:
  1.9 90.9 %shard_map.68 = f32[2,384,1152]{2,1,0:T(8,128)S(1)} custom-call(f32[384,1152]{1,0:T(8,128)} %text_ref.1, f32[384,1152]{1,0:T(8,128)} %image_ref.1, s32[384]{0:T(512)} %mate_ref.1, f32[1]{0:T(128)S(6)} %copy.7.scale_ref, f32[1]{0:T(128)S(6)} %copy.8.offset_ref), custom_call_target="tpu_custom_call" | custom-call | flops 19365101568 | bytes 7077888 | tf_op jit(solution)/shard_map/pallas_call | solution.py:399
  92.9 2.0 %slice_bitcast_fusion = (f32[384,1152]{1,0:T(8,128)}, f32[384,1152]{1,0:T(8,128)}) fusion(f32[2,384,1152]{2,1,0:T(8,128)S(1)} %shard_map.68), kind=kLoop, calls=%fused_computation | loop fusion | bytes 7077888 | tf_op jit(solution)/shard_map/squeeze | solution.py:436

commit v4 on v3

--- a/solution.py
+++ b/solution.py
@@ -326,7 +326,7 @@
             half = item // PIECES
             index = (item - half * PIECES) // 2
             spare = jnp.where((core == side) == (half == 0), X4S, SIB)
-            first = item % 2 == 0
+            first = (item % 2 == 0) != ((half == 1) & (core == side))
             one = jnp.where(half == 0, jnp.where(first, A2, A4), jnp.where(first, B2, B4))
             other = jnp.where(first, jnp.where(half == 0, A2S, B2S), spare)
             kind = jnp.where(

time: 95 us -> 95 us (level)
  no operation moved by 1% of the time
where the time goes in v4:
time: 95 us; the launch traced here: 94.9 us
  Pallas kernels  91 us (96%)
  local copies, waits for them, and re-layouts  2.02 us (2%)
  between operations  1.93 us (2%)
    pallas_call x1, Pallas kernels, body(): pl.pallas_call(functools.partial(kernel, planes), out_shape=pltpu.VMEM((2...  91 us
    squeeze x1, local copies, waits for them, and re-layouts, body(): return (both[0], both[1])  2.02 us

profile of v4, /device:TPU:1, one launch (start us, length us, event | category | flops | bytes accessed | tf_op | source)
XLA Modules:
  0.0 94.9 jit_solution(1350668037352049151)
XLA Ops:
  1.9 91.0 %shard_map.68 = f32[2,384,1152]{2,1,0:T(8,128)S(1)} custom-call(f32[384,1152]{1,0:T(8,128)} %text_ref.1, f32[384,1152]{1,0:T(8,128)} %image_ref.1, s32[384]{0:T(512)} %mate_ref.1, f32[1]{0:T(128)S(6)} %copy.7.scale_ref, f32[1]{0:T(128)S(6)} %copy.8.offset_ref), custom_call_target="tpu_custom_call" | custom-call | flops 19365101568 | bytes 7077888 | tf_op jit(solution)/shard_map/pallas_call | solution.py:399
  92.9 2.0 %slice_bitcast_fusion = (f32[384,1152]{1,0:T(8,128)}, f32[384,1152]{1,0:T(8,128)}) fusion(f32[2,384,1152]{2,1,0:T(8,128)S(1)} %shard_map.68), kind=kLoop, calls=%fused_computation | loop fusion | bytes 7077888 | tf_op jit(solution)/shard_map/squeeze | solution.py:436
